TPU v7x, 512 devices: a whole 4x8x8 slice. The times are simulated.
512 devices in a mesh: gx: 8 (over y), gy: 16 (over z, core), lev: 4 (over x).
Axes of the slice: x: 4, y: 8, z: 8, core: 2. Of those that a mesh axis runs over, the one named last changes fastest.
Arguments:
- wind_x: float32 [128, 256, 2048], P('lev', 'gx', 'gy'), may hold values from -6 to 6
- wind_y: float32 [128, 256, 2048], P('lev', 'gx', 'gy'), may hold values from -6 to 6
- wind_z: float32 [128, 256, 2048], P('lev', 'gx', 'gy'), may hold values from -6 to 6
- pressure: float32 [128, 256, 2048], P('lev', 'gx', 'gy'), may hold values from -6 to 6
- jacobian: float32 [256, 2048], P('gx', 'gy'), may hold values from 0.5 to 2
- slope_x: float32 [256, 2048], P('gx', 'gy'), may hold values from -3 to 3
- slope_y: float32 [256, 2048], P('gx', 'gy'), may hold values from -3 to 3
- stiffness: float32 [128, 256, 2048], P('lev', 'gx', 'gy'), may hold values from 10 to 1000
Outputs:
- wind_x_out: float32 [128, 256, 2048], P('lev', 'gx', 'gy')
- wind_y_out: float32 [128, 256, 2048], P('lev', 'gx', 'gy')
- wind_z_out: float32 [128, 256, 2048], P('lev', 'gx', 'gy')
- pressure_out: float32 [128, 256, 2048], P('lev', 'gx', 'gy')
All inputs are finite; a program needn't handle non-finite values.
Results may differ from a plain program's by a relative error of at most 0.000096.
Values sent between devices are 32-bit elements; how exact they have to be, the bound alone decides.
A program may use at most 64 MiB of HBM per device.

v0:
```python
import jax
import jax.numpy as jnp
from jax import lax
from jax.experimental import pallas as pl
from jax.experimental.pallas import tpu as pltpu
from jax.sharding import PartitionSpec as P

SUBSTEPS = 2
GRAD = 0.35 / 12.0
VERT = 0.25

NZ, NX, NY = 32, 32, 128
GAP = 8
WIDE = NX + 2 * GAP
LEVS = 4
UNROLL = 4
F32 = jnp.float32


def level_rows(ref, row, first=0):
    levels, rows, lanes = ref.shape
    return ref.reshape(levels * rows, lanes), pl.ds(first * rows + row, NZ, stride=rows)


def get_rows(ref, row, first=0):
    flat, there = level_rows(ref, row, first)
    return flat[there, :]


def set_rows(ref, row, value, first=0):
    flat, there = level_rows(ref, row, first)
    flat[there, :] = value


def kernel(
    wx_h, wy_h, wz_h, p_h, j_h, sx_h, sy_h, st_h,
    ox_h, oy_h, oz_h, op_h,
    pbuf, fbuf, wx, wy, wz, ps, st, inv, up_s, q_s, val,
    jac, ijac, slx, sly,
    wyp, npk, jpk, ijpk, nrow,
    ymsg, xmsg, yrecv, xrecv, jprecv, jrecv, strecv,
    vset, vsetrecv, vmsg, vrecv, coef,
    load_sem, store_sem,
    hs_send, hs_recv, ss_send, ss_recv, vs_send, vs_recv, js_send, js_recv, es_send, es_recv,
):
    gx, gy, lev = lax.axis_index("gx"), lax.axis_index("gy"), lax.axis_index("lev")
    ngx, ngy = lax.axis_size("gx"), lax.axis_size("gy")
    xlo, xhi = lax.rem(gx + ngx - 1, ngx), lax.rem(gx + 1, ngx)
    ylo, yhi = lax.rem(gy + ngy - 1, ngy), lax.rem(gy + 1, ngy)
    up, down, over = lax.rem(lev + 1, LEVS), lax.rem(lev + 3, LEVS), lax.rem(lev + 2, LEVS)
    mesh_id = pl.DeviceIdType.MESH

    def remote(src, dst, send, recv, where):
        return pltpu.make_async_remote_copy(
            src_ref=src, dst_ref=dst, send_sem=send, recv_sem=recv,
            device_id=where, device_id_type=mesh_id,
        )

    loads = [
        pltpu.make_async_copy(src, dst, load_sem.at[i])
        for i, (src, dst) in enumerate((
            (p_h, pbuf.at[:, GAP:GAP + NX, :]), (wy_h, wy), (wx_h, wx), (j_h, jac),
            (st_h, st), (sx_h, slx), (sy_h, sly), (wz_h, wz),
        ))
    ]
    for copy in loads:
        copy.start()
    barrier = pltpu.get_barrier_semaphore()
    partners = (
        {"gx": xlo}, {"gx": xhi}, {"gy": ylo}, {"gy": yhi},
        {"lev": up}, {"lev": down}, {"lev": over},
    )
    for where in partners:
        pl.semaphore_signal(barrier, inc=1, device_id=where, device_id_type=mesh_id)

    gap = jnp.zeros((GAP, NY), F32)

    def clear(l, carry):
        pbuf[l, 0:GAP, :] = gap
        pbuf[l, GAP + NX:WIDE, :] = gap
        fbuf[l, 0:GAP, :] = gap
        fbuf[l, GAP + NX:WIDE, :] = gap
        return carry

    lax.fori_loop(0, NZ, clear, 0, unroll=UNROLL)
    ps[0] = jnp.zeros((NX, NY), F32)
    ps[NZ + 1] = jnp.zeros((NX, NY), F32)

    lane = lax.broadcasted_iota(jnp.int32, (1, NY), 1)
    pos, group = lane & 7, lane >> 3

    def at(value, *places):
        hit = pos == places[0]
        for place in places[1:]:
            hit = hit | (pos == place)
        return jnp.where(hit, F32(value), F32(0))

    own_taps = (
        (2, at(1.0, 2, 3, 6, 7)), (1, at(-8.0, 1, 2, 3, 5, 6, 7)),
        (NY - 1, at(8.0, 0, 1, 2, 4, 5, 6)), (NY - 2, at(-1.0, 0, 1, 4, 5)),
    )
    far_taps = (
        (2, at(1.0, 4, 5)), (1, at(-8.0, 4)), (NY - 1, at(8.0, 3)), (NY - 2, at(-1.0, 2, 3)),
    )

    def taps(z, which):
        return sum(c * pltpu.roll(z, s, 1) for s, c in which)

    low_half, inner = pos < 4, (pos >= 2) & (pos <= 5)
    near_edge = (lane < 4) | (lane >= NY - 4)

    def lane_taps(scale):
        return (
            (2, jnp.where(lane >= 2, F32(scale), F32(0))),
            (1, jnp.where(lane >= 1, F32(-8.0 * scale), F32(0))),
            (NY - 1, jnp.where(lane < NY - 1, F32(8.0 * scale), F32(0))),
            (NY - 2, jnp.where(lane < NY - 2, F32(-scale), F32(0))),
        )

    grad_taps, unit_taps = lane_taps(-GRAD), lane_taps(1.0)

    loads[0].wait()
    loads[1].wait()
    acc0 = jnp.zeros((NX, NY), F32)
    for half in range(2):
        def pack(i, carry):
            a, b = carry
            here = group == i
            l = half * 16 + i
            a = jnp.where(here, pltpu.roll(pbuf[l, GAP:GAP + NX, :], 8 * i + 4, 1), a)
            b = jnp.where(here, pltpu.roll(wy[l], (8 * i + 4) , 1), b)
            return a, b

        a, b = lax.fori_loop(0, 15, pack, (acc0, acc0), unroll=5)
        here = group == 15
        a = jnp.where(here, pltpu.roll(pbuf[half * 16 + 15, GAP:GAP + NX, :], 124, 1), a)
        b = jnp.where(here, pltpu.roll(wy[half * 16 + 15], 124, 1), b)
        ymsg[half] = a
        wyp[half] = b

    loads[3].wait()
    j = jac[...]
    ijac[...] = 1.0 / j
    z = jnp.where(lane < 8, pltpu.roll(j, 4, 1), 0.0)
    for shift in (8, 16, 32, 64):
        z = z + pltpu.roll(z, shift, 1)
    jpk[...] = z
    ijpk[...] = 1.0 / z
    loads[2].wait()

    def prow(r):
        return get_rows(pbuf, GAP + r)

    def jrow(r):
        return jac[r:r + 1, :]

    def y_copies(step):
        return (
            remote(ymsg.at[2:4], yrecv.at[step, 0], hs_send.at[0], hs_recv.at[step, 0], {"gy": yhi}),
            remote(ymsg.at[2:4], yrecv.at[step, 1], hs_send.at[1], hs_recv.at[step, 1], {"gy": ylo}),
        )

    def x_copies(step):
        return (
            remote(xmsg.at[1], xrecv.at[step, 0], hs_send.at[2], hs_recv.at[step, 2], {"gx": xhi}),
            remote(xmsg.at[0], xrecv.at[step, 1], hs_send.at[3], hs_recv.at[step, 3], {"gx": xlo}),
        )

    def edges_out(step):
        p0, p1, p2, p3 = (prow(r) for r in range(4))
        p28, p29, p30, p31 = (prow(r) for r in range(NX - 4, NX))
        n0 = get_rows(wx, 0) - GRAD * (8.0 * p1 - p2)
        n1 = get_rows(wx, 1) - GRAD * (8.0 * (p2 - p0) - p3)
        n30 = get_rows(wx, NX - 2) - GRAD * (p28 + 8.0 * (p31 - p29))
        n31 = get_rows(wx, NX - 1) - GRAD * (p29 - 8.0 * p30)
        for i, n in enumerate((n0, n1, n30, n31)):
            nrow[i] = n
        xmsg[0, 0] = p0
        xmsg[0, 1] = p1
        xmsg[0, 2] = jrow(0) * n0
        xmsg[0, 3] = jrow(1) * n1
        xmsg[1, 0] = p30
        xmsg[1, 1] = p31
        xmsg[1, 2] = jrow(NX - 2) * n30
        xmsg[1, 3] = jrow(NX - 1) * n31
        if step == 0:
            pl.semaphore_wait(barrier, len(partners))
        for copy in x_copies(step):
            copy.start()
        jp = jpk[...]
        for half in range(2):
            pp = ymsg[half]
            n = wyp[half] - GRAD * taps(pp, own_taps)
            npk[half] = n
            flux = jp * n
            far = jnp.where(pos < 2, pltpu.roll(flux, NY - 2, 1), pltpu.roll(flux, 2, 1))
            ymsg[2 + half] = jnp.where(inner, pp, far)
        for copy in y_copies(step):
            copy.start()

    def edges_in(step):
        for copy in x_copies(step):
            copy.wait()
        p0, p1, p30, p31 = (xmsg[0, 0], xmsg[0, 1], xmsg[1, 0], xmsg[1, 1])
        low, high = xrecv.at[step, 0], xrecv.at[step, 1]
        jm2, jm1 = jrecv[0, 6:7, :], jrecv[0, 7:8, :]
        j32, j33 = jrecv[1, 0:1, :], jrecv[1, 1:2, :]
        pm2, pm1, p32, p33 = low[0], low[1], high[0], high[1]
        d0 = -GRAD * (pm2 - 8.0 * pm1)
        d1 = -GRAD * pm1
        d30 = GRAD * p32
        d31 = -GRAD * (8.0 * p32 - p33)
        fm2 = low[2] + (GRAD * jm2) * p0
        fm1 = low[3] - (GRAD * jm1) * (8.0 * p0 - p1)
        f32 = high[2] - (GRAD * j32) * (p30 - 8.0 * p31)
        f33 = high[3] - (GRAD * j33) * p31
        g0, g1 = jrow(0) * d0, jrow(1) * d1
        g30, g31 = jrow(NX - 2) * d30, jrow(NX - 1) * d31
        for i, (r, d) in enumerate(((0, d0), (1, d1), (NX - 2, d30), (NX - 1, d31))):
            set_rows(wx, r, nrow[i] + d)
        sums = (
            (0, fm2 + 8.0 * (g1 - fm1)), (1, fm1 - 8.0 * g0), (2, g0 - 8.0 * g1), (3, g1),
            (NX - 4, -g30), (NX - 3, 8.0 * g30 - g31), (NX - 2, 8.0 * g31 - f32),
            (NX - 1, 8.0 * (f32 - g30) - f33),
        )
        for r, s in sums:
            set_rows(ps, r, get_rows(ps, r, 1) - (GRAD * ijac[r:r + 1, :]) * s, 1)

        for copy in y_copies(step):
            copy.wait()
        jp, ijp = jpk[...], ijpk[...]
        jh = jnp.where(low_half, jprecv[0], jprecv[1])
        for half in range(2):
            m = jnp.where(low_half, yrecv[step, 0, half], yrecv[step, 1, half])
            pp = ymsg[half]
            d = -GRAD * taps(m, far_taps)
            part = jnp.where(low_half, pltpu.roll(m, 2, 1), pltpu.roll(m, NY - 2, 1))
            fh = part - GRAD * jh * taps(pp, far_taps)
            s = taps(jp * d, own_taps) + taps(fh, far_taps)
            wyp[half] = npk[half] + d
            dp = (-GRAD) * ijp * s

            def unpack(i, carry):
                l = half * 16 + i
                shift = lax.rem(124 - 8 * i + NY, NY)
                wy[l] = wy[l] + jnp.where(near_edge, pltpu.roll(d, shift, 1), 0.0)
                ps[l + 1] = ps[l + 1] + jnp.where(near_edge, pltpu.roll(dp, shift, 1), 0.0)
                return carry

            lax.fori_loop(0, 16, unpack, 0, unroll=UNROLL)

    def local_step():
        def gradients(l, carry):
            p = pbuf[l, GAP:GAP + NX, :]
            dx = (pbuf[l, GAP - 2:GAP + NX - 2, :] - pbuf[l, GAP + 2:GAP + NX + 2, :]) + 8.0 * (
                pbuf[l, GAP + 1:GAP + NX + 1, :] - pbuf[l, GAP - 1:GAP + NX - 1, :])
            nx = wx[l] - GRAD * dx
            wx[l] = nx
            fbuf[l, GAP:GAP + NX, :] = jac[...] * nx
            wy[l] = wy[l] + taps(p, grad_taps)
            return carry

        lax.fori_loop(0, NZ, gradients, 0, unroll=UNROLL)

        def divergence(l, carry):
            dx = (fbuf[l, GAP - 2:GAP + NX - 2, :] - fbuf[l, GAP + 2:GAP + NX + 2, :]) + 8.0 * (
                fbuf[l, GAP + 1:GAP + NX + 1, :] - fbuf[l, GAP - 1:GAP + NX - 1, :])
            dy = taps(jac[...] * wy[l], unit_taps)
            ps[l + 1] = pbuf[l, GAP:GAP + NX, :] - (GRAD * ijac[...]) * (dx + dy)
            return carry

        lax.fori_loop(0, NZ, divergence, 0, unroll=UNROLL)

    jac_copies = (
        remote(jpk, jprecv.at[0], js_send.at[0], js_recv.at[0], {"gy": yhi}),
        remote(jpk, jprecv.at[1], js_send.at[1], js_recv.at[1], {"gy": ylo}),
        remote(jac.at[NX - 8:NX], jrecv.at[0], js_send.at[2], js_recv.at[2], {"gx": xhi}),
        remote(jac.at[0:8], jrecv.at[1], js_send.at[3], js_recv.at[3], {"gx": xlo}),
    )
    stiff_copies = (
        remote(st.at[NZ - 1], strecv.at[0], es_send.at[0], es_recv.at[0], {"lev": up}),
        remote(st.at[0], strecv.at[1], es_send.at[1], es_recv.at[1], {"lev": down}),
    )
    set_copies = (
        remote(vset, vsetrecv.at[lev], ss_send.at[0], ss_recv.at[0], {"lev": up}),
        remote(vset, vsetrecv.at[lev], ss_send.at[1], ss_recv.at[1], {"lev": down}),
        remote(vset, vsetrecv.at[lev], ss_send.at[2], ss_recv.at[2], {"lev": over}),
    )
    set_arrivals = (
        remote(vset, vsetrecv.at[down], ss_send.at[0], ss_recv.at[0], {"lev": up}),
        remote(vset, vsetrecv.at[up], ss_send.at[1], ss_recv.at[1], {"lev": down}),
        remote(vset, vsetrecv.at[over], ss_send.at[2], ss_recv.at[2], {"lev": over}),
    )

    def v_copies(step, arrivals):
        a, b, c = (down, up, over) if arrivals else (lev, lev, lev)
        return (
            remote(vmsg.at[1:4], vrecv.at[step, a, 1:4], vs_send.at[0], vs_recv.at[step, 0], {"lev": up}),
            remote(vmsg.at[0:3], vrecv.at[step, b, 0:3], vs_send.at[1], vs_recv.at[step, 1], {"lev": down}),
            remote(vmsg.at[1:3], vrecv.at[step, c, 1:3], vs_send.at[2], vs_recv.at[step, 2], {"lev": over}),
        )

    edges_out(0)
    for copy in jac_copies:
        copy.start()
    loads[4].wait()
    for copy in stiff_copies:
        copy.start()

    def factor(i, carry):
        rising, falling = carry
        h = NZ - 1 - i
        inv_l, inv_h = 1.0 / st[i], 1.0 / st[h]
        rising = 1.0 / (2.0 + inv_l - rising)
        falling = 1.0 / (2.0 + inv_h - falling)
        up_s[i] = rising
        val[h] = falling
        return rising, falling

    lax.fori_loop(0, NZ, factor, (acc0, acc0), unroll=UNROLL)

    def spikes(i, carry):
        below, above = carry
        h = NZ - 1 - i
        below = below * val[i]
        above = above * up_s[h]
        val[i] = below
        q_s[h] = above
        inv[i] = 1.0 / st[i]
        return below, above

    ones = jnp.ones((NX, NY), F32)
    lax.fori_loop(0, NZ, spikes, (ones, ones), unroll=UNROLL)
    p_s = st
    vset[0] = val[0]
    vset[1] = q_s[0]
    vset[2] = q_s[NZ - 1]
    for copy in set_copies:
        copy.start()
    for copy in stiff_copies:
        copy.wait()

    def keep(l, carry):
        p_s[l] = val[l]
        return carry

    lax.fori_loop(0, NZ, keep, 0, unroll=UNROLL)

    def after_setup():
        for copy in set_copies:
            copy.wait_send()
        for copy in set_arrivals:
            copy.wait_recv()
        vsetrecv[lev] = vset[...]
        pa = [vsetrecv[i, 0] for i in range(LEVS)]
        qa = [vsetrecv[i, 1] for i in range(LEVS)]
        qb = [vsetrecv[i, 2] for i in range(LEVS)]
        b0 = qb[0]
        t1 = qa[1] / (1.0 - b0 * pa[1])
        b1 = qb[1] + t1 * b0 * qa[1]
        t2 = qa[2] / (1.0 - b1 * pa[2])
        b2 = qb[2] + t2 * b1 * qa[2]
        e3 = pa[3]
        r2 = qa[2] / (1.0 - e3 * qb[2])
        e2 = pa[2] + r2 * e3 * qa[2]
        r1 = qa[1] / (1.0 - e2 * qb[1])
        e1 = pa[1] + r1 * e2 * qa[1]
        z0 = 1.0 / (1.0 - b0 * e1)
        z1 = 1.0 / (1.0 - b1 * e2)
        z2 = 1.0 / (1.0 - b2 * e3)
        for i, c in enumerate((t1, b0, b1, t2, r1, r2, e2, e3, e1, b2, z0, z1, z2)):
            coef[i] = c
        coef[13] = 1.0 / strecv[0]
        coef[14] = 1.0 / strecv[1]

    def pick(*values):
        out = values[-1]
        for i in range(LEVS - 2, -1, -1):
            out = jnp.where(lev == i, values[i], out)
        return out

    for step in range(SUBSTEPS):
        last = step == SUBSTEPS - 1
        if step > 0:
            edges_out(step)
        local_step()
        if step == 0:
            for copy in jac_copies:
                copy.wait()
        edges_in(step)
        if last:
            out_x = pltpu.make_async_copy(wx, ox_h, store_sem.at[0])
            out_y = pltpu.make_async_copy(wy, oy_h, store_sem.at[1])
            out_x.start()
            out_y.start()
        if step == 0:
            for copy in loads[5:]:
                copy.wait()
            after_setup()

        def rising(l, carry):
            v, total = carry
            rhs = wz[l] + slx[...] * wx[l] + sly[...] * wy[l] - VERT * (ps[l + 2] - ps[l])
            rhs = rhs * inv[l]
            total = total + p_s[l] * rhs
            v = (rhs + v) * up_s[l]
            val[l] = v
            return v, total

        top, bottom = lax.fori_loop(0, NZ, rising, (acc0, acc0), unroll=UNROLL)
        vmsg[0] = ps[1]
        vmsg[1] = bottom - VERT * ps[1] * coef[13]
        vmsg[2] = top + VERT * ps[NZ] * coef[14]
        vmsg[3] = ps[NZ]
        for copy in v_copies(step, False):
            copy.start()

        def falling(i, x):
            l = NZ - 2 - i
            x = val[l] + up_s[l] * x
            val[l] = x
            return x

        lax.fori_loop(0, NZ - 1, falling, top, unroll=UNROLL)

        for copy in v_copies(step, False):
            copy.wait_send()
        for copy in v_copies(step, True):
            copy.wait_recv()
        vrecv[step, lev] = vmsg[...]
        ga = [vrecv[step, i, 1] for i in range(LEVS)]
        gb = [vrecv[step, i, 2] for i in range(LEVS)]
        t1, b0, b1, t2, r1, r2, e2, e3, e1, b2, z0, z1, z2 = (coef[i] for i in range(13))
        a0 = gb[0]
        a1 = gb[1] + t1 * (a0 + b0 * ga[1])
        a2 = gb[2] + t2 * (a1 + b1 * ga[2])
        c3 = ga[3]
        c2 = ga[2] + r2 * (c3 + e3 * gb[2])
        c1 = ga[1] + r1 * (c2 + e2 * gb[1])
        w = pick(acc0, (a0 + b0 * c1) * z0, (a1 + b1 * c2) * z1, (a2 + b2 * c3) * z2)
        y = pick((c1 + e1 * a0) * z0, (c2 + e2 * a1) * z1, (c3 + e3 * a2) * z2, acc0)
        under = jnp.where(lev == 0, acc0, w - VERT * vrecv[step, down, 3] * inv[0])
        above = jnp.where(lev == LEVS - 1, acc0, y + VERT * vrecv[step, up, 0] * inv[NZ - 1])

        def solved(l):
            return val[l] + p_s[l] * w + q_s[l] * y

        first = solved(0)
        for half in range(2):
            def finish(i, carry):
                before, here, packed = carry
                l = half * 16 + i
                after = solved(l + 1)
                wz[l] = here
                p = ps[l + 1] - VERT * (after - before)
                pbuf[l, GAP:GAP + NX, :] = p
                if not last:
                    packed = jnp.where(group == i, pltpu.roll(p, lax.rem(8 * i + 4, NY), 1), packed)
                return here, after, packed

            if half == 0:
                carry = lax.fori_loop(0, 16, finish, (under, first, acc0), unroll=UNROLL)
                ymsg[0] = carry[2]
            else:
                before, here, packed = lax.fori_loop(0, 15, finish, (carry[0], carry[1], acc0), unroll=5)
                wz[NZ - 1] = here
                p = ps[NZ] - VERT * (above - before)
                pbuf[NZ - 1, GAP:GAP + NX, :] = p
                ymsg[1] = jnp.where(group == 15, pltpu.roll(p, 124, 1), packed)
    out_z = pltpu.make_async_copy(wz, oz_h, store_sem.at[2])
    out_p = pltpu.make_async_copy(pbuf.at[:, GAP:GAP + NX, :], op_h, store_sem.at[3])
    out_z.start()
    out_p.start()
    out_x.wait()
    out_y.wait()
    out_z.wait()
    out_p.wait()


def local(*blocks):
    whole = jax.ShapeDtypeStruct((NZ, NX, NY), F32)
    anywhere = pl.BlockSpec(memory_space=pl.ANY)

    def vmem(*shape):
        return pltpu.VMEM(shape, F32)

    def dma(*shape):
        return pltpu.SemaphoreType.DMA(shape)

    full, plane = (NZ, NX, NY), (NX, NY)
    return pl.pallas_call(
        kernel,
        out_shape=(whole,) * 4,
        in_specs=[anywhere] * 8,
        out_specs=(anywhere,) * 4,
        scratch_shapes=[
            vmem(NZ, WIDE, NY), vmem(NZ, WIDE, NY),
            vmem(*full), vmem(*full), vmem(*full), vmem(NZ + 2, NX, NY),
            vmem(*full), vmem(*full), vmem(*full), vmem(*full), vmem(*full),
            vmem(*plane), vmem(*plane), vmem(*plane), vmem(*plane),
            vmem(2, *plane), vmem(2, *plane), vmem(*plane), vmem(*plane),
            vmem(4, NZ, NY),
            vmem(4, *plane), vmem(2, 4, NZ, NY),
            vmem(SUBSTEPS, 2, 2, *plane), vmem(SUBSTEPS, 2, 4, NZ, NY),
            vmem(2, *plane), vmem(2, 8, NY), vmem(2, *plane),
            vmem(3, *plane), vmem(LEVS, 3, *plane),
            vmem(4, *plane), vmem(SUBSTEPS, LEVS, 4, *plane), vmem(15, *plane),
            dma(8), dma(4),
            dma(4), dma(SUBSTEPS, 4), dma(3), dma(3), dma(3), dma(SUBSTEPS, 3),
            dma(4), dma(4), dma(2), dma(2),
        ],
        compiler_params=pltpu.CompilerParams(
            collective_id=0, has_side_effects=True, vmem_limit_bytes=40 * 1024 * 1024
        ),
        cost_estimate=pl.CostEstimate(flops=40_000_000, bytes_accessed=5_000_000, transcendentals=0),
    )(*blocks)


def solution(mesh):
    field, column = P("lev", "gx", "gy"), P("gx", "gy")
    return jax.shard_map(
        local,
        mesh=mesh,
        in_specs=(field, field, field, field, column, column, column, field),
        out_specs=(field, field, field, field),
        check_vma=False,
    )
```

profile of v0, /device:TPU:24, one launch (start us, length us, event | category | flops | bytes accessed | tf_op | source)
XLA Modules:
  0.0 46.2 jit_solution(5159310616324048949)
XLA Ops:
  0.6 0.0 copy-start
  0.6 1.0 %copy-done = f32[32,32,128]{2,1,0:T(8,128)S(1)} copy-done((f32[32,32,128]{2,1,0:T(8,128)S(1)}, f32[32,32,128]{2,1,0:T(8,128)}, u32[]{:S(2)}) %copy-start) | copy-done | bytes 524312
  1.7 0.0 copy-start.1
  1.7 1.0 %copy-done.1 = f32[32,32,128]{2,1,0:T(8,128)S(1)} copy-done((f32[32,32,128]{2,1,0:T(8,128)S(1)}, f32[32,32,128]{2,1,0:T(8,128)}, u32[]{:S(2)}) %copy-start.1) | copy-done | bytes 524312
  2.7 0.0 copy-start.2
  2.7 1.0 %copy-done.2 = f32[32,32,128]{2,1,0:T(8,128)S(1)} copy-done((f32[32,32,128]{2,1,0:T(8,128)S(1)}, f32[32,32,128]{2,1,0:T(8,128)}, u32[]{:S(2)}) %copy-start.2) | copy-done | bytes 524312
  3.8 0.0 copy-start.3
  3.8 1.0 %copy-done.3 = f32[32,32,128]{2,1,0:T(8,128)S(1)} copy-done((f32[32,32,128]{2,1,0:T(8,128)S(1)}, f32[32,32,128]{2,1,0:T(8,128)}, u32[]{:S(2)}) %copy-start.3) | copy-done | bytes 524312
  4.8 0.0 copy-start.4
  4.8 1.0 %copy-done.4 = f32[32,32,128]{2,1,0:T(8,128)S(1)} copy-done((f32[32,32,128]{2,1,0:T(8,128)S(1)}, f32[32,32,128]{2,1,0:T(8,128)}, u32[]{:S(2)}) %copy-start.4) | copy-done | bytes 524312
  5.8 0.0 copy-start.5
  5.8 0.7 %copy-done.5 = f32[32,128]{1,0:T(8,128)S(1)} copy-done((f32[32,128]{1,0:T(8,128)S(1)}, f32[32,128]{1,0:T(8,128)}, u32[]{:S(2)}) %copy-start.5) | copy-done | bytes 16408
  6.6 0.0 copy-start.6
  6.6 0.7 %copy-done.6 = f32[32,128]{1,0:T(8,128)S(1)} copy-done((f32[32,128]{1,0:T(8,128)S(1)}, f32[32,128]{1,0:T(8,128)}, u32[]{:S(2)}) %copy-start.6) | copy-done | bytes 16408
  7.3 0.0 copy-start.7
  7.3 0.7 %copy-done.7 = f32[32,128]{1,0:T(8,128)S(1)} copy-done((f32[32,128]{1,0:T(8,128)S(1)}, f32[32,128]{1,0:T(8,128)}, u32[]{:S(2)}) %copy-start.7) | copy-done | bytes 16408
  8.0 35.0 %shard_map.111 = (f32[32,32,128]{2,1,0:T(8,128)S(1)}, f32[32,32,128]{2,1,0:T(8,128)S(1)}, f32[32,32,128]{2,1,0:T(8,128)S(1)}, f32[32,32,128]{2,1,0:T(8,128)S(1)}) custom-call(f32[32,32,128]{2,1,0:T(8,128)S(1)} %copy-done, f32[32,32,128]{2,1,0:T(8,128)S(1)} %copy-done.1, f32[32,32,128]{2,1,0:T(8,128)S(1)} %copy-done.2, f32[32,32,128]{2,1,0:T(8,128)S(1)} %copy-done.3, ...), custom_call_target="tpu_custom_call" | custom-call | flops 40000000 | bytes 5000000 | tf_op jit(solution)/shard_map/pallas_call | solution.py:491
  43.0 0.8 %copy.16 = f32[32,32,128]{2,1,0:T(8,128)} copy(f32[32,32,128]{2,1,0:T(8,128)S(1)} %get-tuple-element.8) | data formatting | bytes 1048576
  43.8 0.8 %copy.17 = f32[32,32,128]{2,1,0:T(8,128)} copy(f32[32,32,128]{2,1,0:T(8,128)S(1)} %get-tuple-element.9) | data formatting | bytes 1048576
  44.6 0.8 %copy.18 = f32[32,32,128]{2,1,0:T(8,128)} copy(f32[32,32,128]{2,1,0:T(8,128)S(1)} %get-tuple-element.10) | data formatting | bytes 1048576
  45.4 0.8 %copy.19 = f32[32,32,128]{2,1,0:T(8,128)} copy(f32[32,32,128]{2,1,0:T(8,128)S(1)} %get-tuple-element.11) | data formatting | bytes 1048576
Async XLA Ops:
  0.6 1.0 %copy-start = (f32[32,32,128]{2,1,0:T(8,128)S(1)}, f32[32,32,128]{2,1,0:T(8,128)}, u32[]{:S(2)}) copy-start(f32[32,32,128]{2,1,0:T(8,128)} %wx_h.1) | copy-start | bytes 1572868
  1.7 1.0 %copy-start.1 = (f32[32,32,128]{2,1,0:T(8,128)S(1)}, f32[32,32,128]{2,1,0:T(8,128)}, u32[]{:S(2)}) copy-start(f32[32,32,128]{2,1,0:T(8,128)} %wy_h.1) | copy-start | bytes 1572868
  2.7 1.0 %copy-start.2 = (f32[32,32,128]{2,1,0:T(8,128)S(1)}, f32[32,32,128]{2,1,0:T(8,128)}, u32[]{:S(2)}) copy-start(f32[32,32,128]{2,1,0:T(8,128)} %wz_h.1) | copy-start | bytes 1572868
  3.8 1.0 %copy-start.3 = (f32[32,32,128]{2,1,0:T(8,128)S(1)}, f32[32,32,128]{2,1,0:T(8,128)}, u32[]{:S(2)}) copy-start(f32[32,32,128]{2,1,0:T(8,128)} %p_h.1) | copy-start | bytes 1572868
  4.8 1.0 %copy-start.4 = (f32[32,32,128]{2,1,0:T(8,128)S(1)}, f32[32,32,128]{2,1,0:T(8,128)}, u32[]{:S(2)}) copy-start(f32[32,32,128]{2,1,0:T(8,128)} %st_h.1) | copy-start | bytes 1572868
  5.8 0.7 %copy-start.5 = (f32[32,128]{1,0:T(8,128)S(1)}, f32[32,128]{1,0:T(8,128)}, u32[]{:S(2)}) copy-start(f32[32,128]{1,0:T(8,128)} %j_h.1) | copy-start | bytes 49156
  6.6 0.7 %copy-start.6 = (f32[32,128]{1,0:T(8,128)S(1)}, f32[32,128]{1,0:T(8,128)}, u32[]{:S(2)}) copy-start(f32[32,128]{1,0:T(8,128)} %sx_h.1) | copy-start | bytes 49156
  7.3 0.7 %copy-start.7 = (f32[32,128]{1,0:T(8,128)S(1)}, f32[32,128]{1,0:T(8,128)}, u32[]{:S(2)}) copy-start(f32[32,128]{1,0:T(8,128)} %sy_h.1) | copy-start | bytes 49156
where the time goes:
time: 46.7 us; the launch traced here: 46.2 us
  Pallas kernels  35 us (75%)
  local copies, waits for them, and re-layouts  10.5 us (22%)
  between operations  0.66 us (1%)
    pallas_call x1, Pallas kernels, local(): pl.pallas_call(kernel, out_shape=(whole,) * 4, in_specs=[anywhere] * 8, o...  35 us
    unnamed x20, local copies, waits for them, and re-layouts  10.5 us

commit v1 on v0

--- a/solution.py
+++ b/solution.py
@@ -13,8 +13,10 @@
 GAP = 8
 WIDE = NX + 2 * GAP
 LEVS = 4
-UNROLL = 4
+UNROLL = 8
 F32 = jnp.float32
+BF16 = jnp.bfloat16
+CHUNK = 4
 
 
 def level_rows(ref, row, first=0):
@@ -33,14 +35,15 @@
 
 
 def kernel(
-    wx_h, wy_h, wz_h, p_h, j_h, sx_h, sy_h, st_h,
-    ox_h, oy_h, oz_h, op_h,
-    pbuf, fbuf, wx, wy, wz, ps, st, inv, up_s, q_s, val,
+    wx_h, wy_h, wz_h, p_h, plane_h, st_h,
+    wx, wy, wz, pout,
+    pbuf, fbuf, ps, st, inv, up_s, q_s, val,
     jac, ijac, slx, sly,
     wyp, npk, jpk, ijpk, nrow,
     ymsg, xmsg, yrecv, xrecv, jprecv, jrecv, strecv,
     vset, vsetrecv, vmsg, vrecv, coef,
-    load_sem, store_sem,
+    pt, qt, pd, qd, wpk, slypk, gsum, dpk, dmat,
+    load_sem,
     hs_send, hs_recv, ss_send, ss_recv, vs_send, vs_recv, js_send, js_recv, es_send, es_recv,
 ):
     gx, gy, lev = lax.axis_index("gx"), lax.axis_index("gy"), lax.axis_index("lev")
@@ -59,8 +62,8 @@
     loads = [
         pltpu.make_async_copy(src, dst, load_sem.at[i])
         for i, (src, dst) in enumerate((
-            (p_h, pbuf.at[:, GAP:GAP + NX, :]), (wy_h, wy), (wx_h, wx), (j_h, jac),
-            (st_h, st), (sx_h, slx), (sy_h, sly), (wz_h, wz),
+            (p_h, pbuf.at[:, GAP:GAP + NX, :]), (wy_h, wy), (wx_h, wx), (plane_h.at[0], jac),
+            (st_h, st), (plane_h.at[1], slx), (plane_h.at[2], sly), (wz_h, wz),
         ))
     ]
     for copy in loads:
@@ -109,44 +112,38 @@
     low_half, inner = pos < 4, (pos >= 2) & (pos <= 5)
     near_edge = (lane < 4) | (lane >= NY - 4)
 
-    def lane_taps(scale):
-        return (
-            (2, jnp.where(lane >= 2, F32(scale), F32(0))),
-            (1, jnp.where(lane >= 1, F32(-8.0 * scale), F32(0))),
-            (NY - 1, jnp.where(lane < NY - 1, F32(8.0 * scale), F32(0))),
-            (NY - 2, jnp.where(lane < NY - 2, F32(-scale), F32(0))),
-        )
-
-    grad_taps, unit_taps = lane_taps(-GRAD), lane_taps(1.0)
-
-    loads[0].wait()
-    loads[1].wait()
+    ahead = lax.broadcasted_iota(jnp.int32, (NY, NY), 0) - lax.broadcasted_iota(jnp.int32, (NY, NY), 1)
+    band = jnp.zeros((NY, NY), F32)
+    for k, c in ((-2, 1.0), (-1, -8.0), (1, 8.0), (2, -1.0)):
+        band = jnp.where(ahead == k, F32(c), band)
+    dmat[0:NY, :] = band.astype(BF16)
+    dmat[NY:2 * NY, :] = band.astype(BF16)
+
+    def lane_diff(f):
+        flat = f.reshape(CHUNK * NX, NY)
+        high = flat.astype(BF16)
+        low = (flat - high.astype(F32)).astype(BF16)
+        both = jnp.concatenate([high, low], axis=1)
+        return jnp.dot(both, dmat[...], preferred_element_type=F32).reshape(CHUNK, NX, NY)
+
     acc0 = jnp.zeros((NX, NY), F32)
-    for half in range(2):
-        def pack(i, carry):
-            a, b = carry
-            here = group == i
-            l = half * 16 + i
-            a = jnp.where(here, pltpu.roll(pbuf[l, GAP:GAP + NX, :], 8 * i + 4, 1), a)
-            b = jnp.where(here, pltpu.roll(wy[l], (8 * i + 4) , 1), b)
-            return a, b
-
-        a, b = lax.fori_loop(0, 15, pack, (acc0, acc0), unroll=5)
-        here = group == 15
-        a = jnp.where(here, pltpu.roll(pbuf[half * 16 + 15, GAP:GAP + NX, :], 124, 1), a)
-        b = jnp.where(here, pltpu.roll(wy[half * 16 + 15], 124, 1), b)
-        ymsg[half] = a
-        wyp[half] = b
-
-    loads[3].wait()
-    j = jac[...]
-    ijac[...] = 1.0 / j
-    z = jnp.where(lane < 8, pltpu.roll(j, 4, 1), 0.0)
-    for shift in (8, 16, 32, 64):
-        z = z + pltpu.roll(z, shift, 1)
-    jpk[...] = z
-    ijpk[...] = 1.0 / z
-    loads[2].wait()
+    def pack(sources):
+        out = []
+        for half in range(2):
+            carry = [acc0] * len(sources)
+            for i in range(16):
+                here = group == i
+                for k, src in enumerate(sources):
+                    turned = pltpu.roll(src(half * 16 + i), (8 * i + 4) % NY, 1)
+                    carry[k] = jnp.where(here, turned, carry[k])
+            out.append(carry)
+        return tuple(zip(*out))
+
+    def spread_out(plane):
+        z = jnp.where(lane < 8, pltpu.roll(plane, 4, 1), 0.0)
+        for shift in (8, 16, 32, 64):
+            z = z + pltpu.roll(z, shift, 1)
+        return z
 
     def prow(r):
         return get_rows(pbuf, GAP + r)
@@ -167,6 +164,10 @@
         )
 
     def edges_out(step):
+        if step == 0:
+            loads[0].wait()
+            loads[2].wait()
+            loads[3].wait()
         p0, p1, p2, p3 = (prow(r) for r in range(4))
         p28, p29, p30, p31 = (prow(r) for r in range(NX - 4, NX))
         n0 = get_rows(wx, 0) - GRAD * (8.0 * p1 - p2)
@@ -187,6 +188,17 @@
             pl.semaphore_wait(barrier, len(partners))
         for copy in x_copies(step):
             copy.start()
+        pressure = lambda l: pbuf[l, GAP:GAP + NX, :]
+        if step == 0:
+            jpk[...] = spread_out(jac[...])
+            loads[1].wait()
+            packed = pack((pressure, lambda l: wy[l]))
+            for half in range(2):
+                wyp[half] = packed[1][half]
+        else:
+            packed = pack((pressure,))
+        for half in range(2):
+            ymsg[half] = packed[0][half]
         jp = jpk[...]
         for half in range(2):
             pp = ymsg[half]
@@ -216,19 +228,27 @@
         f33 = high[3] - (GRAD * j33) * p31
         g0, g1 = jrow(0) * d0, jrow(1) * d1
         g30, g31 = jrow(NX - 2) * d30, jrow(NX - 1) * d31
-        for i, (r, d) in enumerate(((0, d0), (1, d1), (NX - 2, d30), (NX - 1, d31))):
-            set_rows(wx, r, nrow[i] + d)
+        delta = {0: d0, 1: d1, NX - 2: d30, NX - 1: d31}
+        for i, r in enumerate(delta):
+            set_rows(wx, r, nrow[i] + delta[r])
         sums = (
             (0, fm2 + 8.0 * (g1 - fm1)), (1, fm1 - 8.0 * g0), (2, g0 - 8.0 * g1), (3, g1),
             (NX - 4, -g30), (NX - 3, 8.0 * g30 - g31), (NX - 2, 8.0 * g31 - f32),
             (NX - 1, 8.0 * (f32 - g30) - f33),
         )
         for r, s in sums:
-            set_rows(ps, r, get_rows(ps, r, 1) - (GRAD * ijac[r:r + 1, :]) * s, 1)
+            dp = (-GRAD * ijac[r:r + 1, :]) * s
+            set_rows(ps, r, get_rows(ps, r, 1) + dp, 1)
+            for side, (near, far) in enumerate(((pt, pd), (qt, qd))):
+                change = get_rows(far, r) * dp
+                if r in delta:
+                    change = change + get_rows(near, r, 1) * (slx[r:r + 1, :] * delta[r])
+                gsum[side, r:r + 1, :] = gsum[side, r:r + 1, :] + jnp.sum(change, axis=0, keepdims=True)
 
         for copy in y_copies(step):
             copy.wait()
         jp, ijp = jpk[...], ijpk[...]
+        change = [acc0, acc0]
         jh = jnp.where(low_half, jprecv[0], jprecv[1])
         for half in range(2):
             m = jnp.where(low_half, yrecv[step, 0, half], yrecv[step, 1, half])
@@ -239,37 +259,62 @@
             s = taps(jp * d, own_taps) + taps(fh, far_taps)
             wyp[half] = npk[half] + d
             dp = (-GRAD) * ijp * s
-
+            dpk[0, half], dpk[1, half] = d, dp
+            sd = slypk[...] * d
+            change = [c + wpk[k, half] * sd + wpk[k + 2, half] * dp for k, c in enumerate(change)]
+        for side in range(2):
+            total = change[side]
+            for shift in (8, 16, 32, 64):
+                total = total + pltpu.roll(total, shift, 1)
+            gsum[side] = gsum[side] + jnp.where(near_edge, pltpu.roll(total, 124, 1), 0.0)
+        unpack_level(0, 0, 124)
+        unpack_level(1, 15, 4)
+
+    def unpack_level(half, i, shift):
+        l = half * 16 + i
+        wy[l] = wy[l] + jnp.where(near_edge, pltpu.roll(dpk[0, half], shift, 1), 0.0)
+        ps[l + 1] = ps[l + 1] + jnp.where(near_edge, pltpu.roll(dpk[1, half], shift, 1), 0.0)
+
+    def unpack_rest():
+        for half in range(2):
             def unpack(i, carry):
-                l = half * 16 + i
-                shift = lax.rem(124 - 8 * i + NY, NY)
-                wy[l] = wy[l] + jnp.where(near_edge, pltpu.roll(d, shift, 1), 0.0)
-                ps[l + 1] = ps[l + 1] + jnp.where(near_edge, pltpu.roll(dp, shift, 1), 0.0)
+                unpack_level(half, i, lax.rem(124 - 8 * i + NY, NY))
                 return carry
 
-            lax.fori_loop(0, 16, unpack, 0, unroll=UNROLL)
+            lax.fori_loop(1 - half, 16 - half, unpack, 0, unroll=5)
+
+    def pre_source(l):
+        return wz[l] + slx[...] * wx[l] + sly[...] * wy[l] - VERT * (ps[l + 2] - ps[l])
+
+    def block_ends():
+        def add(l, carry):
+            rhs = pre_source(l)
+            return carry[0] + pt[l + 1] * rhs, carry[1] + qt[l + 1] * rhs
+
+        gsum[0], gsum[1] = lax.fori_loop(0, NZ, add, (acc0, acc0), unroll=UNROLL)
 
     def local_step():
-        def gradients(l, carry):
-            p = pbuf[l, GAP:GAP + NX, :]
-            dx = (pbuf[l, GAP - 2:GAP + NX - 2, :] - pbuf[l, GAP + 2:GAP + NX + 2, :]) + 8.0 * (
-                pbuf[l, GAP + 1:GAP + NX + 1, :] - pbuf[l, GAP - 1:GAP + NX - 1, :])
-            nx = wx[l] - GRAD * dx
-            wx[l] = nx
-            fbuf[l, GAP:GAP + NX, :] = jac[...] * nx
-            wy[l] = wy[l] + taps(p, grad_taps)
+        def row_diff(ref, lv):
+            at_row = lambda k: ref[lv, GAP + k:GAP + NX + k, :]
+            return (at_row(-2) - at_row(2)) + 8.0 * (at_row(1) - at_row(-1))
+
+        def gradients(i, carry):
+            lv = pl.ds(i * CHUNK, CHUNK)
+            nx = wx[lv] - GRAD * row_diff(pbuf, lv)
+            wx[lv] = nx
+            fbuf[lv, GAP:GAP + NX, :] = jac[...] * nx
+            wy[lv] = wy[lv] - GRAD * lane_diff(pbuf[lv, GAP:GAP + NX, :])
             return carry
 
-        lax.fori_loop(0, NZ, gradients, 0, unroll=UNROLL)
-
-        def divergence(l, carry):
-            dx = (fbuf[l, GAP - 2:GAP + NX - 2, :] - fbuf[l, GAP + 2:GAP + NX + 2, :]) + 8.0 * (
-                fbuf[l, GAP + 1:GAP + NX + 1, :] - fbuf[l, GAP - 1:GAP + NX - 1, :])
-            dy = taps(jac[...] * wy[l], unit_taps)
-            ps[l + 1] = pbuf[l, GAP:GAP + NX, :] - (GRAD * ijac[...]) * (dx + dy)
+        lax.fori_loop(0, NZ // CHUNK, gradients, 0, unroll=2)
+
+        def divergence(i, carry):
+            lv = pl.ds(i * CHUNK, CHUNK)
+            spread = row_diff(fbuf, lv) + lane_diff(jac[...] * wy[lv])
+            ps[pl.ds(i * CHUNK + 1, CHUNK)] = pbuf[lv, GAP:GAP + NX, :] - (GRAD * ijac[...]) * spread
             return carry
 
-        lax.fori_loop(0, NZ, divergence, 0, unroll=UNROLL)
+        lax.fori_loop(0, NZ // CHUNK, divergence, 0, unroll=2)
 
     jac_copies = (
         remote(jpk, jprecv.at[0], js_send.at[0], js_recv.at[0], {"gy": yhi}),
@@ -340,11 +385,29 @@
     for copy in stiff_copies:
         copy.wait()
 
-    def keep(l, carry):
+    pt[0] = qt[0] = pt[NZ + 1] = qt[NZ + 1] = acc0
+
+    def weigh(l, carry):
         p_s[l] = val[l]
+        pt[l + 1] = val[l] * inv[l]
+        qt[l + 1] = q_s[l] * inv[l]
         return carry
 
-    lax.fori_loop(0, NZ, keep, 0, unroll=UNROLL)
+    lax.fori_loop(0, NZ, weigh, 0, unroll=UNROLL)
+
+    def weigh_apart(l, carry):
+        pd[l] = VERT * (pt[l + 2] - pt[l])
+        qd[l] = VERT * (qt[l + 2] - qt[l])
+        return carry
+
+    lax.fori_loop(0, NZ, weigh_apart, 0, unroll=UNROLL)
+    coef[13] = 1.0 / strecv[0]
+    coef[14] = 1.0 / strecv[1]
+    ijac[...] = 1.0 / jac[...]
+    ijpk[...] = 1.0 / jpk[...]
+    for copy in loads[5:]:
+        copy.wait()
+    slypk[...] = spread_out(sly[...])
 
     def after_setup():
         for copy in set_copies:
@@ -370,8 +433,6 @@
         z2 = 1.0 / (1.0 - b2 * e3)
         for i, c in enumerate((t1, b0, b1, t2, r1, r2, e2, e3, e1, b2, z0, z1, z2)):
             coef[i] = c
-        coef[13] = 1.0 / strecv[0]
-        coef[14] = 1.0 / strecv[1]
 
     def pick(*values):
         out = values[-1]
@@ -384,36 +445,29 @@
         if step > 0:
             edges_out(step)
         local_step()
+        block_ends()
         if step == 0:
+            packed = pack((lambda l: pt[l + 1], lambda l: qt[l + 1], lambda l: pd[l], lambda l: qd[l]))
+            for k in range(4):
+                for half in range(2):
+                    wpk[k, half] = packed[k][half]
             for copy in jac_copies:
                 copy.wait()
         edges_in(step)
-        if last:
-            out_x = pltpu.make_async_copy(wx, ox_h, store_sem.at[0])
-            out_y = pltpu.make_async_copy(wy, oy_h, store_sem.at[1])
-            out_x.start()
-            out_y.start()
-        if step == 0:
-            for copy in loads[5:]:
-                copy.wait()
-            after_setup()
-
-        def rising(l, carry):
-            v, total = carry
-            rhs = wz[l] + slx[...] * wx[l] + sly[...] * wy[l] - VERT * (ps[l + 2] - ps[l])
-            rhs = rhs * inv[l]
-            total = total + p_s[l] * rhs
-            v = (rhs + v) * up_s[l]
-            val[l] = v
-            return v, total
-
-        top, bottom = lax.fori_loop(0, NZ, rising, (acc0, acc0), unroll=UNROLL)
         vmsg[0] = ps[1]
-        vmsg[1] = bottom - VERT * ps[1] * coef[13]
-        vmsg[2] = top + VERT * ps[NZ] * coef[14]
+        vmsg[1] = gsum[0] - VERT * ps[1] * coef[13]
+        vmsg[2] = gsum[1] + VERT * ps[NZ] * coef[14]
         vmsg[3] = ps[NZ]
         for copy in v_copies(step, False):
             copy.start()
+        unpack_rest()
+
+        def rising(l, v):
+            v = (pre_source(l) * inv[l] + v) * up_s[l]
+            val[l] = v
+            return v
+
+        top = lax.fori_loop(0, NZ, rising, acc0, unroll=UNROLL)
 
         def falling(i, x):
             l = NZ - 2 - i
@@ -422,6 +476,8 @@
             return x
 
         lax.fori_loop(0, NZ - 1, falling, top, unroll=UNROLL)
+        if step == 0:
+            after_setup()
 
         for copy in v_copies(step, False):
             copy.wait_send()
@@ -445,41 +501,36 @@
         def solved(l):
             return val[l] + p_s[l] * w + q_s[l] * y
 
-        first = solved(0)
-        for half in range(2):
-            def finish(i, carry):
-                before, here, packed = carry
-                l = half * 16 + i
-                after = solved(l + 1)
-                wz[l] = here
-                p = ps[l + 1] - VERT * (after - before)
+        def keep_pressure(l, p):
+            if last:
+                pout[l] = p
+            else:
                 pbuf[l, GAP:GAP + NX, :] = p
-                if not last:
-                    packed = jnp.where(group == i, pltpu.roll(p, lax.rem(8 * i + 4, NY), 1), packed)
-                return here, after, packed
-
-            if half == 0:
-                carry = lax.fori_loop(0, 16, finish, (under, first, acc0), unroll=UNROLL)
-                ymsg[0] = carry[2]
-            else:
-                before, here, packed = lax.fori_loop(0, 15, finish, (carry[0], carry[1], acc0), unroll=5)
-                wz[NZ - 1] = here
-                p = ps[NZ] - VERT * (above - before)
-                pbuf[NZ - 1, GAP:GAP + NX, :] = p
-                ymsg[1] = jnp.where(group == 15, pltpu.roll(p, 124, 1), packed)
-    out_z = pltpu.make_async_copy(wz, oz_h, store_sem.at[2])
-    out_p = pltpu.make_async_copy(pbuf.at[:, GAP:GAP + NX, :], op_h, store_sem.at[3])
-    out_z.start()
-    out_p.start()
-    out_x.wait()
-    out_y.wait()
-    out_z.wait()
-    out_p.wait()
+
+        def finish(l, carry):
+            before, here = carry
+            after = solved(l + 1)
+            wz[l] = here
+            keep_pressure(l, ps[l + 1] - VERT * (after - before))
+            return here, after
+
+        before, here = lax.fori_loop(0, NZ - 1, finish, (under, solved(0)), unroll=UNROLL)
+        wz[NZ - 1] = here
+        keep_pressure(NZ - 1, ps[NZ] - VERT * (above - before))
+
+
+def store(*refs):
+    sems = refs[-1]
+    copies = [pltpu.make_async_copy(refs[i], refs[4 + i], sems.at[i]) for i in range(4)]
+    for copy in copies:
+        copy.start()
+    for copy in copies:
+        copy.wait()
 
 
 def local(*blocks):
     whole = jax.ShapeDtypeStruct((NZ, NX, NY), F32)
-    anywhere = pl.BlockSpec(memory_space=pl.ANY)
+    anywhere, hbm = pl.BlockSpec(memory_space=pl.ANY), pl.BlockSpec(memory_space=pltpu.HBM)
 
     def vmem(*shape):
         return pltpu.VMEM(shape, F32)
@@ -488,14 +539,14 @@
         return pltpu.SemaphoreType.DMA(shape)
 
     full, plane = (NZ, NX, NY), (NX, NY)
-    return pl.pallas_call(
+    blocks = pl.pallas_call(
         kernel,
         out_shape=(whole,) * 4,
-        in_specs=[anywhere] * 8,
-        out_specs=(anywhere,) * 4,
+        in_specs=[hbm] * 6,
+        out_specs=(pl.BlockSpec(memory_space=pltpu.VMEM),) * 4,
         scratch_shapes=[
             vmem(NZ, WIDE, NY), vmem(NZ, WIDE, NY),
-            vmem(*full), vmem(*full), vmem(*full), vmem(NZ + 2, NX, NY),
+            vmem(NZ + 2, NX, NY),
             vmem(*full), vmem(*full), vmem(*full), vmem(*full), vmem(*full),
             vmem(*plane), vmem(*plane), vmem(*plane), vmem(*plane),
             vmem(2, *plane), vmem(2, *plane), vmem(*plane), vmem(*plane),
@@ -505,14 +556,25 @@
             vmem(2, *plane), vmem(2, 8, NY), vmem(2, *plane),
             vmem(3, *plane), vmem(LEVS, 3, *plane),
             vmem(4, *plane), vmem(SUBSTEPS, LEVS, 4, *plane), vmem(15, *plane),
-            dma(8), dma(4),
+            vmem(NZ + 2, NX, NY), vmem(NZ + 2, NX, NY), vmem(*full), vmem(*full),
+            vmem(4, 2, *plane), vmem(*plane), vmem(2, *plane), vmem(2, 2, *plane),
+            pltpu.VMEM((2 * NY, NY), BF16),
+            dma(8),
             dma(4), dma(SUBSTEPS, 4), dma(3), dma(3), dma(3), dma(SUBSTEPS, 3),
             dma(4), dma(4), dma(2), dma(2),
         ],
         compiler_params=pltpu.CompilerParams(
-            collective_id=0, has_side_effects=True, vmem_limit_bytes=40 * 1024 * 1024
+            collective_id=0, has_side_effects=True, vmem_limit_bytes=53000 * 1024
         ),
-        cost_estimate=pl.CostEstimate(flops=40_000_000, bytes_accessed=5_000_000, transcendentals=0),
+    )(*blocks[:4], jnp.stack(blocks[4:7]), blocks[7])
+    return pl.pallas_call(
+        store,
+        out_shape=(whole,) * 4,
+        in_specs=[anywhere] * 4,
+        out_specs=(hbm,) * 4,
+        scratch_shapes=[dma(4)],
+        compiler_params=pltpu.CompilerParams(vmem_limit_bytes=1024 * 1024),
+        cost_estimate=pl.CostEstimate(flops=0, bytes_accessed=4_000_000, transcendentals=0),
     )(*blocks)
 
 

time: 46.7 us -> 37.3 us (0.80)
  local copies, waits for them, and re-layouts: 10.5 us -> 0 us
  other arithmetic: 0 us -> 0.76 us
  Pallas kernels: 35 us -> 35.6 us
    unnamed x20 -> x0, local copies, waits for them, and re-layouts: 10.5 us -> none
    another operation x0 -> x1, other arithmetic: none -> 0.76 us  [local(): jnp.stack(blocks[4:7])]
    pallas_call x1 -> x2, Pallas kernels: 35 us -> 35.6 us  [the longest x1 34.2 us: local(): pl.pallas_call(kernel, out_shape=(whole,) * 4, in_specs=[hbm] * 6, out_sp...]
where the time goes in v1:
time: 37.3 us; the launch traced here: 37 us
  Pallas kernels  35.6 us (95%)
  other arithmetic  0.76 us (2%)
  between operations  0.64 us (2%)
    pallas_call x1, Pallas kernels, local(): pl.pallas_call(kernel, out_shape=(whole,) * 4, in_specs=[hbm] * 6, out_sp...  34.2 us
    pallas_call x1, Pallas kernels, local(): pl.pallas_call(store, out_shape=(whole,) * 4, in_specs=[anywhere] * 4, ou...  1.35 us
    another operation x1, other arithmetic, local(): jnp.stack(blocks[4:7])  0.76 us

profile of v1, /device:TPU:24, one launch (start us, length us, event | category | flops | bytes accessed | tf_op | source)
XLA Modules:
  0.0 37.0 jit_solution(2339313405290667264)
XLA Ops:
  0.6 0.8 %pad_maximum_fusion.plane_h = f32[3,32,128]{2,1,0:T(8,128)S(1)} fusion(f32[1,32,128]{2,1,0:T(8,128)} %bitcast.3, f32[1,32,128]{2,1,0:T(8,128)} %bitcast.4, f32[1,32,128]{2,1,0:T(8,128)} %bitcast.5), kind=kLoop, calls=%fused_computation | loop fusion | flops 24576 | bytes 98304 | tf_op jit(solution)/shard_map/stack | solution.py:569
  1.4 34.2 %shard_map.111 = (f32[32,32,128]{2,1,0:T(8,128)S(1)}, f32[32,32,128]{2,1,0:T(8,128)S(1)}, f32[32,32,128]{2,1,0:T(8,128)S(1)}, f32[32,32,128]{2,1,0:T(8,128)S(1)}) custom-call(f32[32,32,128]{2,1,0:T(8,128)} %wx_h.1, f32[32,32,128]{2,1,0:T(8,128)} %wy_h.1, f32[32,32,128]{2,1,0:T(8,128)} %wz_h.1, f32[32,32,128]{2,1,0:T(8,128)} %p_h.1, ...), custom_call_target="tpu_custom_call" | custom-call | tf_op jit(solution)/shard_map/pallas_call | solution.py:542
  35.6 1.3 %shard_map.112 = (f32[32,32,128]{2,1,0:T(8,128)}, f32[32,32,128]{2,1,0:T(8,128)}, f32[32,32,128]{2,1,0:T(8,128)}, f32[32,32,128]{2,1,0:T(8,128)}) custom-call(f32[32,32,128]{2,1,0:T(8,128)S(1)} %get-tuple-element.8.refs_0_, f32[32,32,128]{2,1,0:T(8,128)S(1)} %get-tuple-element.9.refs_1_, f32[32,32,128]{2,1,0:T(8,128)S(1)} %get-tuple-element.10.refs_2_, ...), custom_call_target="tpu_custom_call" | custom-call | bytes 4000000 | tf_op jit(solution)/shard_map/pallas_call | solution.py:570

commit v2 on v1

--- a/solution.py
+++ b/solution.py
@@ -17,6 +17,8 @@
 F32 = jnp.float32
 BF16 = jnp.bfloat16
 CHUNK = 4
+EDGE_ROWS = (0, 1, 2, 3, NX - 4, NX - 3, NX - 2, NX - 1)
+FLUX_ROWS = (0, 1, NX - 2, NX - 1)
 
 
 def level_rows(ref, row, first=0):
@@ -42,7 +44,7 @@
     wyp, npk, jpk, ijpk, nrow,
     ymsg, xmsg, yrecv, xrecv, jprecv, jrecv, strecv,
     vset, vsetrecv, vmsg, vrecv, coef,
-    pt, qt, pd, qd, wpk, slypk, gsum, dpk, dmat,
+    pt, qt, pd, qd, wpk, slypk, gsum, dpk, dmat, p_s, xw, dpx, farp,
     load_sem,
     hs_send, hs_recv, ss_send, ss_recv, vs_send, vs_recv, js_send, js_recv, es_send, es_recv,
 ):
@@ -106,6 +108,11 @@
         (2, at(1.0, 4, 5)), (1, at(-8.0, 4)), (NY - 1, at(8.0, 3)), (NY - 2, at(-1.0, 2, 3)),
     )
 
+    flux_taps = (
+        (2, at(1.0, 4, 5), at(1.0, 2, 3)), (1, at(-8.0, 2, 4, 5), at(-8.0, 3)),
+        (NY - 1, at(8.0, 2, 3, 5), at(8.0, 4)), (NY - 2, at(-1.0, 2, 3), at(-1.0, 4, 5)),
+    )
+
     def taps(z, which):
         return sum(c * pltpu.roll(z, s, 1) for s, c in which)
 
@@ -170,10 +177,11 @@
             loads[3].wait()
         p0, p1, p2, p3 = (prow(r) for r in range(4))
         p28, p29, p30, p31 = (prow(r) for r in range(NX - 4, NX))
-        n0 = get_rows(wx, 0) - GRAD * (8.0 * p1 - p2)
-        n1 = get_rows(wx, 1) - GRAD * (8.0 * (p2 - p0) - p3)
-        n30 = get_rows(wx, NX - 2) - GRAD * (p28 + 8.0 * (p31 - p29))
-        n31 = get_rows(wx, NX - 1) - GRAD * (p29 - 8.0 * p30)
+        wind_row = lambda i: nrow[i] if step else get_rows(wx, FLUX_ROWS[i])
+        n0 = wind_row(0) - GRAD * (8.0 * p1 - p2)
+        n1 = wind_row(1) - GRAD * (8.0 * (p2 - p0) - p3)
+        n30 = wind_row(2) - GRAD * (p28 + 8.0 * (p31 - p29))
+        n31 = wind_row(3) - GRAD * (p29 - 8.0 * p30)
         for i, n in enumerate((n0, n1, n30, n31)):
             nrow[i] = n
         xmsg[0, 0] = p0
@@ -188,6 +196,8 @@
             pl.semaphore_wait(barrier, len(partners))
         for copy in x_copies(step):
             copy.start()
+        if step == 0:
+            columns()
         pressure = lambda l: pbuf[l, GAP:GAP + NX, :]
         if step == 0:
             jpk[...] = spread_out(jac[...])
@@ -209,6 +219,11 @@
             ymsg[2 + half] = jnp.where(inner, pp, far)
         for copy in y_copies(step):
             copy.start()
+        far_parts()
+
+    def far_parts():
+        for half in range(2):
+            farp[half] = taps(ymsg[half], far_taps)
 
     def edges_in(step):
         for copy in x_copies(step):
@@ -229,20 +244,21 @@
         g0, g1 = jrow(0) * d0, jrow(1) * d1
         g30, g31 = jrow(NX - 2) * d30, jrow(NX - 1) * d31
         delta = {0: d0, 1: d1, NX - 2: d30, NX - 1: d31}
-        for i, r in enumerate(delta):
-            set_rows(wx, r, nrow[i] + delta[r])
+        for i, r in enumerate(FLUX_ROWS):
+            nrow[i] = nrow[i] + delta[r]
         sums = (
-            (0, fm2 + 8.0 * (g1 - fm1)), (1, fm1 - 8.0 * g0), (2, g0 - 8.0 * g1), (3, g1),
-            (NX - 4, -g30), (NX - 3, 8.0 * g30 - g31), (NX - 2, 8.0 * g31 - f32),
-            (NX - 1, 8.0 * (f32 - g30) - f33),
+            fm2 + 8.0 * (g1 - fm1), fm1 - 8.0 * g0, g0 - 8.0 * g1, g1,
+            -g30, 8.0 * g30 - g31, 8.0 * g31 - f32, 8.0 * (f32 - g30) - f33,
         )
-        for r, s in sums:
+        for i, (r, s) in enumerate(zip(EDGE_ROWS, sums)):
             dp = (-GRAD * ijac[r:r + 1, :]) * s
-            set_rows(ps, r, get_rows(ps, r, 1) + dp, 1)
-            for side, (near, far) in enumerate(((pt, pd), (qt, qd))):
-                change = get_rows(far, r) * dp
+            dpx[i] = dp
+            ps[1, r:r + 1, :] = ps[1, r:r + 1, :] + dp[0:1, :]
+            ps[NZ, r:r + 1, :] = ps[NZ, r:r + 1, :] + dp[NZ - 1:NZ, :]
+            for side in range(2):
+                change = xw[side, i] * dp
                 if r in delta:
-                    change = change + get_rows(near, r, 1) * (slx[r:r + 1, :] * delta[r])
+                    change = change + xw[side, 8 + FLUX_ROWS.index(r)] * delta[r]
                 gsum[side, r:r + 1, :] = gsum[side, r:r + 1, :] + jnp.sum(change, axis=0, keepdims=True)
 
         for copy in y_copies(step):
@@ -252,11 +268,14 @@
         jh = jnp.where(low_half, jprecv[0], jprecv[1])
         for half in range(2):
             m = jnp.where(low_half, yrecv[step, 0, half], yrecv[step, 1, half])
-            pp = ymsg[half]
-            d = -GRAD * taps(m, far_taps)
-            part = jnp.where(low_half, pltpu.roll(m, 2, 1), pltpu.roll(m, NY - 2, 1))
-            fh = part - GRAD * jh * taps(pp, far_taps)
-            s = taps(jp * d, own_taps) + taps(fh, far_taps)
+            turned = [pltpu.roll(m, k, 1) for k, _ in far_taps]
+            d = -GRAD * sum(c * t for (_, c), t in zip(far_taps, turned))
+            fh = jnp.where(low_half, turned[0], turned[3]) - GRAD * jh * farp[half]
+            g = jp * d
+            s = sum(
+                pltpu.roll(jnp.where(inner, own * g + far * fh, 0.0), k, 1)
+                for k, own, far in flux_taps
+            )
             wyp[half] = npk[half] + d
             dp = (-GRAD) * ijp * s
             dpk[0, half], dpk[1, half] = d, dp
@@ -337,59 +356,56 @@
         remote(vset, vsetrecv.at[over], ss_send.at[2], ss_recv.at[2], {"lev": over}),
     )
 
-    def v_copies(step, arrivals):
-        a, b, c = (down, up, over) if arrivals else (lev, lev, lev)
+    def v_copies(step):
         return (
-            remote(vmsg.at[1:4], vrecv.at[step, a, 1:4], vs_send.at[0], vs_recv.at[step, 0], {"lev": up}),
-            remote(vmsg.at[0:3], vrecv.at[step, b, 0:3], vs_send.at[1], vs_recv.at[step, 1], {"lev": down}),
-            remote(vmsg.at[1:3], vrecv.at[step, c, 1:3], vs_send.at[2], vs_recv.at[step, 2], {"lev": over}),
+            remote(vmsg.at[3:5], vrecv.at[step, 0], vs_send.at[0], vs_recv.at[step, 0], {"lev": up}),
+            remote(vmsg.at[0:2], vrecv.at[step, 1], vs_send.at[1], vs_recv.at[step, 1], {"lev": down}),
+            remote(vmsg.at[2:3], vrecv.at[step, 2, 0:1], vs_send.at[2], vs_recv.at[step, 2], {"lev": over}),
         )
+
+    def columns():
+        loads[4].wait()
+        for copy in stiff_copies:
+            copy.start()
+
+        def factor(i, carry):
+            rising, falling = carry
+            h = NZ - 1 - i
+            inv_l, inv_h = 1.0 / st[i], 1.0 / st[h]
+            rising = 1.0 / (2.0 + inv_l - rising)
+            falling = 1.0 / (2.0 + inv_h - falling)
+            up_s[i] = rising
+            val[h] = falling
+            return rising, falling
+
+        lax.fori_loop(0, NZ, factor, (acc0, acc0), unroll=UNROLL)
+
+        def spikes(i, carry):
+            below, above = carry
+            h = NZ - 1 - i
+            below = below * val[i]
+            above = above * up_s[h]
+            p_s[i] = below
+            q_s[h] = above
+            inv[i] = 1.0 / st[i]
+            return below, above
+
+        ones = jnp.ones((NX, NY), F32)
+        lax.fori_loop(0, NZ, spikes, (ones, ones), unroll=UNROLL)
+        vset[0] = p_s[0]
+        vset[1] = q_s[0]
+        vset[2] = q_s[NZ - 1]
+        for copy in set_copies:
+            copy.start()
 
     edges_out(0)
     for copy in jac_copies:
         copy.start()
-    loads[4].wait()
-    for copy in stiff_copies:
-        copy.start()
-
-    def factor(i, carry):
-        rising, falling = carry
-        h = NZ - 1 - i
-        inv_l, inv_h = 1.0 / st[i], 1.0 / st[h]
-        rising = 1.0 / (2.0 + inv_l - rising)
-        falling = 1.0 / (2.0 + inv_h - falling)
-        up_s[i] = rising
-        val[h] = falling
-        return rising, falling
-
-    lax.fori_loop(0, NZ, factor, (acc0, acc0), unroll=UNROLL)
-
-    def spikes(i, carry):
-        below, above = carry
-        h = NZ - 1 - i
-        below = below * val[i]
-        above = above * up_s[h]
-        val[i] = below
-        q_s[h] = above
-        inv[i] = 1.0 / st[i]
-        return below, above
-
-    ones = jnp.ones((NX, NY), F32)
-    lax.fori_loop(0, NZ, spikes, (ones, ones), unroll=UNROLL)
-    p_s = st
-    vset[0] = val[0]
-    vset[1] = q_s[0]
-    vset[2] = q_s[NZ - 1]
-    for copy in set_copies:
-        copy.start()
-    for copy in stiff_copies:
-        copy.wait()
 
     pt[0] = qt[0] = pt[NZ + 1] = qt[NZ + 1] = acc0
 
     def weigh(l, carry):
-        p_s[l] = val[l]
-        pt[l + 1] = val[l] * inv[l]
+        pt[l + 1] = p_s[l] * inv[l]
         qt[l + 1] = q_s[l] * inv[l]
         return carry
 
@@ -401,13 +417,20 @@
         return carry
 
     lax.fori_loop(0, NZ, weigh_apart, 0, unroll=UNROLL)
-    coef[13] = 1.0 / strecv[0]
-    coef[14] = 1.0 / strecv[1]
     ijac[...] = 1.0 / jac[...]
     ijpk[...] = 1.0 / jpk[...]
     for copy in loads[5:]:
         copy.wait()
     slypk[...] = spread_out(sly[...])
+
+    depth = lax.broadcasted_iota(jnp.int32, (NZ, NY), 0)
+    inside = (depth > 0) & (depth < NZ - 1)
+
+    def pick(*values):
+        out = values[-1]
+        for i in range(LEVS - 2, -1, -1):
+            out = jnp.where(lev == i, values[i], out)
+        return out
 
     def after_setup():
         for copy in set_copies:
@@ -433,12 +456,8 @@
         z2 = 1.0 / (1.0 - b2 * e3)
         for i, c in enumerate((t1, b0, b1, t2, r1, r2, e2, e3, e1, b2, z0, z1, z2)):
             coef[i] = c
-
-    def pick(*values):
-        out = values[-1]
-        for i in range(LEVS - 2, -1, -1):
-            out = jnp.where(lev == i, values[i], out)
-        return out
+        coef[15] = pick(acc0, t1 * b0, t2 * b1, acc0)
+        coef[16] = pick(acc0, r1 * e2, r2 * e3, acc0)
 
     for step in range(SUBSTEPS):
         last = step == SUBSTEPS - 1
@@ -451,15 +470,34 @@
             for k in range(4):
                 for half in range(2):
                     wpk[k, half] = packed[k][half]
-            for copy in jac_copies:
+            for side, (near, far) in enumerate(((pt, pd), (qt, qd))):
+                for i, r in enumerate(EDGE_ROWS):
+                    xw[side, i] = get_rows(far, r)
+                for i, r in enumerate(FLUX_ROWS):
+                    xw[side, 8 + i] = slx[r:r + 1, :] * get_rows(near, r, 1)
+            for copy in jac_copies + stiff_copies:
                 copy.wait()
+            coef[13] = 1.0 / strecv[0]
+            coef[14] = 1.0 / strecv[1]
+            after_setup()
         edges_in(step)
+        ga = gsum[0] - VERT * ps[1] * coef[13]
+        gb = gsum[1] + VERT * ps[NZ] * coef[14]
+        own_mu = gb + coef[15] * ga
+        own_nu = ga + coef[16] * gb
         vmsg[0] = ps[1]
-        vmsg[1] = gsum[0] - VERT * ps[1] * coef[13]
-        vmsg[2] = gsum[1] + VERT * ps[NZ] * coef[14]
-        vmsg[3] = ps[NZ]
-        for copy in v_copies(step, False):
+        vmsg[1] = jnp.where(lev == 0, own_mu, own_nu)
+        vmsg[2] = jnp.where(lev < 2, own_mu, own_nu)
+        vmsg[3] = jnp.where(lev == LEVS - 1, own_nu, own_mu)
+        vmsg[4] = ps[NZ]
+        for copy in v_copies(step):
             copy.start()
+        gsum[0], gsum[1] = own_mu, own_nu
+        for i, r in enumerate(FLUX_ROWS):
+            set_rows(wx, r, nrow[i])
+        for i, r in enumerate(EDGE_ROWS):
+            there = dpx[i]
+            set_rows(ps, r, get_rows(ps, r, 1) + jnp.where(inside, there, 0.0), 1)
         unpack_rest()
 
         def rising(l, v):
@@ -476,27 +514,21 @@
             return x
 
         lax.fori_loop(0, NZ - 1, falling, top, unroll=UNROLL)
-        if step == 0:
-            after_setup()
-
-        for copy in v_copies(step, False):
-            copy.wait_send()
-        for copy in v_copies(step, True):
-            copy.wait_recv()
-        vrecv[step, lev] = vmsg[...]
-        ga = [vrecv[step, i, 1] for i in range(LEVS)]
-        gb = [vrecv[step, i, 2] for i in range(LEVS)]
+        for copy in v_copies(step):
+            copy.wait()
+        own_mu, own_nu = gsum[0], gsum[1]
+        low, high, far = vrecv[step, 0, 0], vrecv[step, 1, 1], vrecv[step, 2, 0]
         t1, b0, b1, t2, r1, r2, e2, e3, e1, b2, z0, z1, z2 = (coef[i] for i in range(13))
-        a0 = gb[0]
-        a1 = gb[1] + t1 * (a0 + b0 * ga[1])
-        a2 = gb[2] + t2 * (a1 + b1 * ga[2])
-        c3 = ga[3]
-        c2 = ga[2] + r2 * (c3 + e3 * gb[2])
-        c1 = ga[1] + r1 * (c2 + e2 * gb[1])
+        a0 = pick(own_mu, low, far, high)
+        a1 = pick(acc0, own_mu, low, far) + t1 * a0
+        a2 = pick(acc0, acc0, own_mu, low) + t2 * a1
+        c3 = pick(low, far, high, own_nu)
+        c2 = pick(far, high, own_nu, acc0) + r2 * c3
+        c1 = pick(high, own_nu, acc0, acc0) + r1 * c2
         w = pick(acc0, (a0 + b0 * c1) * z0, (a1 + b1 * c2) * z1, (a2 + b2 * c3) * z2)
         y = pick((c1 + e1 * a0) * z0, (c2 + e2 * a1) * z1, (c3 + e3 * a2) * z2, acc0)
-        under = jnp.where(lev == 0, acc0, w - VERT * vrecv[step, down, 3] * inv[0])
-        above = jnp.where(lev == LEVS - 1, acc0, y + VERT * vrecv[step, up, 0] * inv[NZ - 1])
+        under = jnp.where(lev == 0, acc0, w - VERT * vrecv[step, 0, 1] * inv[0])
+        above = jnp.where(lev == LEVS - 1, acc0, y + VERT * vrecv[step, 1, 0] * inv[NZ - 1])
 
         def solved(l):
             return val[l] + p_s[l] * w + q_s[l] * y
@@ -555,10 +587,11 @@
             vmem(SUBSTEPS, 2, 2, *plane), vmem(SUBSTEPS, 2, 4, NZ, NY),
             vmem(2, *plane), vmem(2, 8, NY), vmem(2, *plane),
             vmem(3, *plane), vmem(LEVS, 3, *plane),
-            vmem(4, *plane), vmem(SUBSTEPS, LEVS, 4, *plane), vmem(15, *plane),
+            vmem(5, *plane), vmem(SUBSTEPS, 3, 2, *plane), vmem(17, *plane),
             vmem(NZ + 2, NX, NY), vmem(NZ + 2, NX, NY), vmem(*full), vmem(*full),
             vmem(4, 2, *plane), vmem(*plane), vmem(2, *plane), vmem(2, 2, *plane),
-            pltpu.VMEM((2 * NY, NY), BF16),
+            pltpu.VMEM((2 * NY, NY), BF16), vmem(*full),
+            vmem(2, 12, NZ, NY), vmem(8, NZ, NY), vmem(2, *plane),
             dma(8),
             dma(4), dma(SUBSTEPS, 4), dma(3), dma(3), dma(3), dma(SUBSTEPS, 3),
             dma(4), dma(4), dma(2), dma(2),

time: 37.3 us -> 33.4 us (0.90)
  Pallas kernels: 35.6 us -> 31.7 us
    pallas_call x1, Pallas kernels: 34.2 us -> 30.3 us  [local(): pl.pallas_call(kernel, out_shape=(whole,) * 4, in_specs=[hbm] * 6, out_sp...]
where the time goes in v2:
time: 33.4 us; the launch traced here: 33.1 us
  Pallas kernels  31.7 us (95%)
  other arithmetic  0.76 us (2%)
  between operations  0.64 us (2%)
    pallas_call x1, Pallas kernels, local(): pl.pallas_call(kernel, out_shape=(whole,) * 4, in_specs=[hbm] * 6, out_sp...  30.3 us
    pallas_call x1, Pallas kernels, local(): pl.pallas_call(store, out_shape=(whole,) * 4, in_specs=[anywhere] * 4, ou...  1.35 us
    another operation x1, other arithmetic, local(): jnp.stack(blocks[4:7])  0.76 us

profile of v2, /device:TPU:24, one launch (start us, length us, event | category | flops | bytes accessed | tf_op | source)
XLA Modules:
  0.0 33.1 jit_solution(17295993153968614793)
XLA Ops:
  0.6 0.8 %pad_maximum_fusion.plane_h = f32[3,32,128]{2,1,0:T(8,128)S(1)} fusion(f32[1,32,128]{2,1,0:T(8,128)} %bitcast.3, f32[1,32,128]{2,1,0:T(8,128)} %bitcast.4, f32[1,32,128]{2,1,0:T(8,128)} %bitcast.5), kind=kLoop, calls=%fused_computation | loop fusion | flops 24576 | bytes 98304 | tf_op jit(solution)/shard_map/stack | solution.py:602
  1.4 30.3 %shard_map.111 = (f32[32,32,128]{2,1,0:T(8,128)S(1)}, f32[32,32,128]{2,1,0:T(8,128)S(1)}, f32[32,32,128]{2,1,0:T(8,128)S(1)}, f32[32,32,128]{2,1,0:T(8,128)S(1)}) custom-call(f32[32,32,128]{2,1,0:T(8,128)} %wx_h.1, f32[32,32,128]{2,1,0:T(8,128)} %wy_h.1, f32[32,32,128]{2,1,0:T(8,128)} %wz_h.1, f32[32,32,128]{2,1,0:T(8,128)} %p_h.1, ...), custom_call_target="tpu_custom_call" | custom-call | tf_op jit(solution)/shard_map/pallas_call | solution.py:574
  31.7 1.3 %shard_map.112 = (f32[32,32,128]{2,1,0:T(8,128)}, f32[32,32,128]{2,1,0:T(8,128)}, f32[32,32,128]{2,1,0:T(8,128)}, f32[32,32,128]{2,1,0:T(8,128)}) custom-call(f32[32,32,128]{2,1,0:T(8,128)S(1)} %get-tuple-element.8.refs_0_, f32[32,32,128]{2,1,0:T(8,128)S(1)} %get-tuple-element.9.refs_1_, f32[32,32,128]{2,1,0:T(8,128)S(1)} %get-tuple-element.10.refs_2_, ...), custom_call_target="tpu_custom_call" | custom-call | bytes 4000000 | tf_op jit(solution)/shard_map/pallas_call | solution.py:603

commit v3 on v2

--- a/solution.py
+++ b/solution.py
@@ -37,7 +37,7 @@
 
 
 def kernel(
-    wx_h, wy_h, wz_h, p_h, plane_h, st_h,
+    wx_h, wy_h, wz_h, p_h, j_h, sx_h, sy_h, st_h,
     wx, wy, wz, pout,
     pbuf, fbuf, ps, st, inv, up_s, q_s, val,
     jac, ijac, slx, sly,
@@ -64,12 +64,10 @@
     loads = [
         pltpu.make_async_copy(src, dst, load_sem.at[i])
         for i, (src, dst) in enumerate((
-            (p_h, pbuf.at[:, GAP:GAP + NX, :]), (wy_h, wy), (wx_h, wx), (plane_h.at[0], jac),
-            (st_h, st), (plane_h.at[1], slx), (plane_h.at[2], sly), (wz_h, wz),
+            (p_h, pbuf.at[:, GAP:GAP + NX, :]), (wy_h, wy), (wx_h, wx), (j_h, jac),
+            (st_h, st), (sx_h, slx), (sy_h, sly), (wz_h, wz),
         ))
     ]
-    for copy in loads:
-        copy.start()
     barrier = pltpu.get_barrier_semaphore()
     partners = (
         {"gx": xlo}, {"gx": xhi}, {"gy": ylo}, {"gy": yhi},
@@ -77,6 +75,8 @@
     )
     for where in partners:
         pl.semaphore_signal(barrier, inc=1, device_id=where, device_id_type=mesh_id)
+    for copy in loads:
+        copy.start()
 
     gap = jnp.zeros((GAP, NY), F32)
 
@@ -226,6 +226,34 @@
             farp[half] = taps(ymsg[half], far_taps)
 
     def edges_in(step):
+        for copy in y_copies(step):
+            copy.wait()
+        jp, ijp = jpk[...], ijpk[...]
+        change = [acc0, acc0]
+        jh = jnp.where(low_half, jprecv[0], jprecv[1])
+        for half in range(2):
+            m = jnp.where(low_half, yrecv[step, 0, half], yrecv[step, 1, half])
+            turned = [pltpu.roll(m, k, 1) for k, _ in far_taps]
+            d = -GRAD * sum(c * t for (_, c), t in zip(far_taps, turned))
+            fh = jnp.where(low_half, turned[0], turned[3]) - GRAD * jh * farp[half]
+            g = jp * d
+            s = sum(
+                pltpu.roll(jnp.where(inner, own * g + far * fh, 0.0), k, 1)
+                for k, own, far in flux_taps
+            )
+            wyp[half] = npk[half] + d
+            dp = (-GRAD) * ijp * s
+            dpk[0, half], dpk[1, half] = d, dp
+            sd = slypk[...] * d
+            change = [c + wpk[k, half] * sd + wpk[k + 2, half] * dp for k, c in enumerate(change)]
+        for side in range(2):
+            total = change[side]
+            for shift in (8, 16, 32, 64):
+                total = total + pltpu.roll(total, shift, 1)
+            gsum[side] = gsum[side] + jnp.where(near_edge, pltpu.roll(total, 124, 1), 0.0)
+        unpack_level(0, 0, 124)
+        unpack_level(1, 15, 4)
+
         for copy in x_copies(step):
             copy.wait()
         p0, p1, p30, p31 = (xmsg[0, 0], xmsg[0, 1], xmsg[1, 0], xmsg[1, 1])
@@ -260,34 +288,6 @@
                 if r in delta:
                     change = change + xw[side, 8 + FLUX_ROWS.index(r)] * delta[r]
                 gsum[side, r:r + 1, :] = gsum[side, r:r + 1, :] + jnp.sum(change, axis=0, keepdims=True)
-
-        for copy in y_copies(step):
-            copy.wait()
-        jp, ijp = jpk[...], ijpk[...]
-        change = [acc0, acc0]
-        jh = jnp.where(low_half, jprecv[0], jprecv[1])
-        for half in range(2):
-            m = jnp.where(low_half, yrecv[step, 0, half], yrecv[step, 1, half])
-            turned = [pltpu.roll(m, k, 1) for k, _ in far_taps]
-            d = -GRAD * sum(c * t for (_, c), t in zip(far_taps, turned))
-            fh = jnp.where(low_half, turned[0], turned[3]) - GRAD * jh * farp[half]
-            g = jp * d
-            s = sum(
-                pltpu.roll(jnp.where(inner, own * g + far * fh, 0.0), k, 1)
-                for k, own, far in flux_taps
-            )
-            wyp[half] = npk[half] + d
-            dp = (-GRAD) * ijp * s
-            dpk[0, half], dpk[1, half] = d, dp
-            sd = slypk[...] * d
-            change = [c + wpk[k, half] * sd + wpk[k + 2, half] * dp for k, c in enumerate(change)]
-        for side in range(2):
-            total = change[side]
-            for shift in (8, 16, 32, 64):
-                total = total + pltpu.roll(total, shift, 1)
-            gsum[side] = gsum[side] + jnp.where(near_edge, pltpu.roll(total, 124, 1), 0.0)
-        unpack_level(0, 0, 124)
-        unpack_level(1, 15, 4)
 
     def unpack_level(half, i, shift):
         l = half * 16 + i
@@ -574,7 +574,7 @@
     blocks = pl.pallas_call(
         kernel,
         out_shape=(whole,) * 4,
-        in_specs=[hbm] * 6,
+        in_specs=[hbm] * 8,
         out_specs=(pl.BlockSpec(memory_space=pltpu.VMEM),) * 4,
         scratch_shapes=[
             vmem(NZ, WIDE, NY), vmem(NZ, WIDE, NY),
@@ -597,9 +597,9 @@
             dma(4), dma(4), dma(2), dma(2),
         ],
         compiler_params=pltpu.CompilerParams(
-            collective_id=0, has_side_effects=True, vmem_limit_bytes=53000 * 1024
+            collective_id=0, has_side_effects=True, vmem_limit_bytes=40 * 1024 * 1024
         ),
-    )(*blocks[:4], jnp.stack(blocks[4:7]), blocks[7])
+    )(*[pltpu.with_memory_space_constraint(b, pltpu.HBM) for b in blocks])
     return pl.pallas_call(
         store,
         out_shape=(whole,) * 4,

time: 33.4 us -> 31.9 us (0.955)
  other arithmetic: 0.76 us -> 0 us
  Pallas kernels: 31.7 us -> 31.1 us
    another operation x1 -> x0, other arithmetic: 0.76 us -> none  [local(): jnp.stack(blocks[4:7])]
    pallas_call x1, Pallas kernels: 30.3 us -> 29.8 us  [local(): pl.pallas_call(kernel, out_shape=(whole,) * 4, in_specs=[hbm] * 8, out_sp...]
where the time goes in v3:
time: 31.9 us; the launch traced here: 31.8 us
  Pallas kernels  31.1 us (97%)
  between operations  0.64 us (2%)
    pallas_call x1, Pallas kernels, local(): pl.pallas_call(kernel, out_shape=(whole,) * 4, in_specs=[hbm] * 8, out_sp...  29.8 us
    pallas_call x1, Pallas kernels, local(): pl.pallas_call(store, out_shape=(whole,) * 4, in_specs=[anywhere] * 4, ou...  1.35 us

profile of v3, /device:TPU:24, one launch (start us, length us, event | category | flops | bytes accessed | tf_op | source)
XLA Modules:
  0.0 31.8 jit_solution(6072561891642630376)
XLA Ops:
  0.6 29.8 %shard_map.111 = (f32[32,32,128]{2,1,0:T(8,128)S(1)}, f32[32,32,128]{2,1,0:T(8,128)S(1)}, f32[32,32,128]{2,1,0:T(8,128)S(1)}, f32[32,32,128]{2,1,0:T(8,128)S(1)}) custom-call(f32[32,32,128]{2,1,0:T(8,128)} %wx_h.1, f32[32,32,128]{2,1,0:T(8,128)} %wy_h.1, f32[32,32,128]{2,1,0:T(8,128)} %wz_h.1, f32[32,32,128]{2,1,0:T(8,128)} %p_h.1, f32[32,128]{1,0:T(8,128)} %j_h.1, ...), custom_call_target="tpu_custom_call" | custom-call | tf_op jit(solution)/shard_map/pallas_call | solution.py:574
  30.4 1.3 %shard_map.112 = (f32[32,32,128]{2,1,0:T(8,128)}, f32[32,32,128]{2,1,0:T(8,128)}, f32[32,32,128]{2,1,0:T(8,128)}, f32[32,32,128]{2,1,0:T(8,128)}) custom-call(f32[32,32,128]{2,1,0:T(8,128)S(1)} %get-tuple-element.8.refs_0_, f32[32,32,128]{2,1,0:T(8,128)S(1)} %get-tuple-element.9.refs_1_, f32[32,32,128]{2,1,0:T(8,128)S(1)} %get-tuple-element.10.refs_2_, ...), custom_call_target="tpu_custom_call" | custom-call | bytes 4000000 | tf_op jit(solution)/shard_map/pallas_call | solution.py:603

commit v4 on v3

--- a/solution.py
+++ b/solution.py
@@ -44,7 +44,7 @@
     wyp, npk, jpk, ijpk, nrow,
     ymsg, xmsg, yrecv, xrecv, jprecv, jrecv, strecv,
     vset, vsetrecv, vmsg, vrecv, coef,
-    pt, qt, pd, qd, wpk, slypk, gsum, dpk, dmat, p_s, xw, dpx, farp,
+    pt, qt, pd, qd, wpk, slypk, gsum, dpk, dmat, p_s, xw, dpx, farp, erow, ends,
     load_sem,
     hs_send, hs_recv, ss_send, ss_recv, vs_send, vs_recv, js_send, js_recv, es_send, es_recv,
 ):
@@ -170,13 +170,12 @@
             remote(xmsg.at[0], xrecv.at[step, 1], hs_send.at[3], hs_recv.at[step, 3], {"gx": xlo}),
         )
 
-    def edges_out(step):
+    def rows_out(step, rows):
         if step == 0:
             loads[0].wait()
             loads[2].wait()
             loads[3].wait()
-        p0, p1, p2, p3 = (prow(r) for r in range(4))
-        p28, p29, p30, p31 = (prow(r) for r in range(NX - 4, NX))
+        p0, p1, p2, p3, p28, p29, p30, p31 = rows()
         wind_row = lambda i: nrow[i] if step else get_rows(wx, FLUX_ROWS[i])
         n0 = wind_row(0) - GRAD * (8.0 * p1 - p2)
         n1 = wind_row(1) - GRAD * (8.0 * (p2 - p0) - p3)
@@ -198,6 +197,8 @@
             copy.start()
         if step == 0:
             columns()
+
+    def columns_out(step):
         pressure = lambda l: pbuf[l, GAP:GAP + NX, :]
         if step == 0:
             jpk[...] = spread_out(jac[...])
@@ -398,7 +399,8 @@
         for copy in set_copies:
             copy.start()
 
-    edges_out(0)
+    rows_out(0, lambda: [prow(r) for r in EDGE_ROWS])
+    columns_out(0)
     for copy in jac_copies:
         copy.start()
 
@@ -462,7 +464,7 @@
     for step in range(SUBSTEPS):
         last = step == SUBSTEPS - 1
         if step > 0:
-            edges_out(step)
+            columns_out(step)
         local_step()
         block_ends()
         if step == 0:
@@ -514,6 +516,10 @@
             return x
 
         lax.fori_loop(0, NZ - 1, falling, top, unroll=UNROLL)
+        if not last:
+            for i, r in enumerate(EDGE_ROWS):
+                for k, value in enumerate((get_rows(val, r), get_rows(ps, r, 1), get_rows(p_s, r), get_rows(q_s, r))):
+                    erow[k, i] = value
         for copy in v_copies(step):
             copy.wait()
         own_mu, own_nu = gsum[0], gsum[1]
@@ -529,6 +535,22 @@
         y = pick((c1 + e1 * a0) * z0, (c2 + e2 * a1) * z1, (c3 + e3 * a2) * z2, acc0)
         under = jnp.where(lev == 0, acc0, w - VERT * vrecv[step, 0, 1] * inv[0])
         above = jnp.where(lev == LEVS - 1, acc0, y + VERT * vrecv[step, 1, 0] * inv[NZ - 1])
+
+        if not last:
+            for k, value in enumerate((w, y, under, above)):
+                ends[k] = value
+
+            def new_rows():
+                out = []
+                for i, r in enumerate(EDGE_ROWS):
+                    w_r, y_r, under_r, above_r = (ends[k, r:r + 1, :] for k in range(4))
+                    x = erow[0, i] + erow[2, i] * w_r + erow[3, i] * y_r
+                    before = jnp.where(depth == 0, under_r, pltpu.roll(x, 1, 0))
+                    after = jnp.where(depth == NZ - 1, above_r, pltpu.roll(x, NZ - 1, 0))
+                    out.append(erow[1, i] - VERT * (after - before))
+                return out
+
+            rows_out(step + 1, new_rows)
 
         def solved(l):
             return val[l] + p_s[l] * w + q_s[l] * y
@@ -592,6 +614,7 @@
             vmem(4, 2, *plane), vmem(*plane), vmem(2, *plane), vmem(2, 2, *plane),
             pltpu.VMEM((2 * NY, NY), BF16), vmem(*full),
             vmem(2, 12, NZ, NY), vmem(8, NZ, NY), vmem(2, *plane),
+            vmem(4, 8, NZ, NY), vmem(4, *plane),
             dma(8),
             dma(4), dma(SUBSTEPS, 4), dma(3), dma(3), dma(3), dma(SUBSTEPS, 3),
             dma(4), dma(4), dma(2), dma(2),

time: 31.9 us -> 31.7 us (level)
  no operation moved by 1% of the time
where the time goes in v4:
time: 31.7 us; the launch traced here: 31.6 us
  Pallas kernels  30.9 us (97%)
  between operations  0.64 us (2%)
    pallas_call x1, Pallas kernels, local(): pl.pallas_call(kernel, out_shape=(whole,) * 4, in_specs=[hbm] * 8, out_sp...  29.6 us
    pallas_call x1, Pallas kernels, local(): pl.pallas_call(store, out_shape=(whole,) * 4, in_specs=[anywhere] * 4, ou...  1.35 us

profile of v4, /device:TPU:24, one launch (start us, length us, event | category | flops | bytes accessed | tf_op | source)
XLA Modules:
  0.0 31.6 jit_solution(12889050345698868186)
XLA Ops:
  0.6 29.6 %shard_map.111 = (f32[32,32,128]{2,1,0:T(8,128)S(1)}, f32[32,32,128]{2,1,0:T(8,128)S(1)}, f32[32,32,128]{2,1,0:T(8,128)S(1)}, f32[32,32,128]{2,1,0:T(8,128)S(1)}) custom-call(f32[32,32,128]{2,1,0:T(8,128)} %wx_h.1, f32[32,32,128]{2,1,0:T(8,128)} %wy_h.1, f32[32,32,128]{2,1,0:T(8,128)} %wz_h.1, f32[32,32,128]{2,1,0:T(8,128)} %p_h.1, f32[32,128]{1,0:T(8,128)} %j_h.1, ...), custom_call_target="tpu_custom_call" | custom-call | tf_op jit(solution)/shard_map/pallas_call | solution.py:596
  30.2 1.3 %shard_map.112 = (f32[32,32,128]{2,1,0:T(8,128)}, f32[32,32,128]{2,1,0:T(8,128)}, f32[32,32,128]{2,1,0:T(8,128)}, f32[32,32,128]{2,1,0:T(8,128)}) custom-call(f32[32,32,128]{2,1,0:T(8,128)S(1)} %get-tuple-element.8.refs_0_, f32[32,32,128]{2,1,0:T(8,128)S(1)} %get-tuple-element.9.refs_1_, f32[32,32,128]{2,1,0:T(8,128)S(1)} %get-tuple-element.10.refs_2_, ...), custom_call_target="tpu_custom_call" | custom-call | bytes 4000000 | tf_op jit(solution)/shard_map/pallas_call | solution.py:626
